TPU v7x, 512 devices: a whole 4x4x16 slice. The times are simulated.
512 devices in a mesh: space: 64 (over z_lo, x, core), batch: 8 (over z_hi, y).
Axes of the slice: x: 4, y: 4, z: 16 (z_hi: 2, z_lo: 8; z = z_hi * 8 + z_lo), core: 2. Of those that a mesh axis runs over, the one named last changes fastest.
Arguments:
- fine_parts: bfloat16 [8, 32768, 128], P('batch', 'space'), may hold values from -5 to 5
- parent_parts: bfloat16 [8, 4096, 128], P('batch', 'space'), may hold values from -5 to 5
- coarse_local: float32 [4096, 128], P('space'), may hold values from -6 to 6
- fine_source: int32 [189, 32768], P(None, 'space'), may hold values from 0 to 159
- fine_operator: int32 [189, 32768], P(None, 'space'), may hold values from 0 to 63
- parent_source: int32 [189, 4096], P(None, 'space'), may hold values from 0 to 159
- parent_operator: int32 [189, 4096], P(None, 'space'), may hold values from 0 to 63
- operators: bfloat16 [64, 128, 128], replicated, may hold values from -0.0390625 to 0.0390625
- child_shift: bfloat16 [8, 128, 128], replicated, may hold values from -0.5 to 0.5
- basis: bfloat16 [32768, 128, 128], P('space', 'batch'), may hold values from -0.5 to 0.5
- counts: int32 [8, 32768], P('batch', 'space'), may hold values from 1 to 16
Outputs:
- potential: float32 [128, 32768], P('batch', 'space')
Inputs may be any that keep to these rules, and one draw needn't show every extreme that they name: `fine_source`: an entry v names, in the target's own block if v // 32 is 0 and else in the block whose index differs from the target's in bit v // 32 - 1, box v % 32 of the aligned group of 32 boxes that holds the target's position. `parent_source`: an entry v names, in the target's own block if v // 32 is 0 and else in the block whose index differs from the target's in bit v // 32 - 1, parent box v % 32 of the aligned group of 32 parent boxes that holds the target's position.
All inputs are finite; a program needn't handle non-finite values.
Results may differ from a plain program's by a relative error of at most 0.015.
Values may be sent and summed in bfloat16 or wider, within the bound.
A program may use at most 64 MiB of HBM per device.

v0:
```python
import math
import jax
import jax.numpy as jnp
from jax import lax
from jax.sharding import PartitionSpec as P

NTERMS = 121
WINDOW = 32


def partner(shard, axis, apart):
    return lax.ppermute(shard, axis, [(i, i ^ 1 << apart) for i in range(lax.axis_size(axis))])


def far_field(stacked, source_list, operator_list, operators, row_start):
    kind_count, coef_width, _ = operators.shape
    flat_ops = operators.reshape(kind_count * coef_width, coef_width)
    list_length, total_rows = source_list.shape
    piece_rows = math.gcd(total_rows, WINDOW)
    piece_count = total_rows // piece_rows
    source_pieces = source_list.reshape(list_length, piece_count, piece_rows).transpose(1, 0, 2)
    kind_pieces = operator_list.reshape(list_length, piece_count, piece_rows).transpose(1, 0, 2)
    starts = row_start + lax.iota(jnp.int32, piece_count) * piece_rows
    kinds_iota = lax.iota(jnp.int32, kind_count)
    column_iota = lax.iota(jnp.int32, stacked.shape[0] * WINDOW)

    def one_piece(pieces):
        sources, kinds, start = pieces
        corner = start // WINDOW * WINDOW
        nearby = lax.dynamic_slice_in_dim(stacked, corner, WINDOW, 1).reshape(-1, coef_width)
        chosen = (sources[:, :, None] == column_iota).astype(jnp.bfloat16)
        onehot = (kinds[:, :, None] == kinds_iota).astype(jnp.bfloat16)
        counted = jnp.einsum(
            "jbt,jbr->btr", onehot, chosen, preferred_element_type=jnp.float32
        ).astype(jnp.bfloat16)
        grouped = jnp.einsum(
            "btr,rk->btk", counted, nearby, preferred_element_type=jnp.float32
        ).astype(jnp.bfloat16)
        return jnp.dot(
            grouped.reshape(piece_rows, kind_count * coef_width),
            flat_ops,
            preferred_element_type=jnp.float32,
        )

    return lax.map(one_piece, (source_pieces, kind_pieces, starts)).reshape(total_rows, coef_width)


def with_partners(fine_mult, parent_mult):
    fine_blocks = [fine_mult]
    parent_blocks = [parent_mult]
    for bit_number in range(4):
        fine_other, parent_other = partner((fine_mult, parent_mult), "space", bit_number)
        fine_blocks.append(fine_other)
        parent_blocks.append(parent_other)
    return (jnp.stack(fine_blocks), jnp.stack(parent_blocks))


def children(parent_local, fine_far, child_shift):
    shifted = jnp.einsum(
        "pk,okl->pol", parent_local, child_shift, preferred_element_type=jnp.float32
    )
    whole = shifted.reshape(fine_far.shape) + fine_far
    keep = lax.iota(jnp.int32, whole.shape[1]) < NTERMS
    return jnp.where(keep[None, :], whole, 0.0).astype(jnp.bfloat16)


def body(
    fine_parts,
    parent_parts,
    coarse_local,
    fine_source,
    fine_operator,
    parent_source,
    parent_operator,
    operators,
    child_shift,
    basis,
    counts,
):
    fine_terms = fine_parts[0].astype(jnp.float32)
    parent_terms = parent_parts[0].astype(jnp.float32)
    fine_total, parent_total = (
        lax.psum(fine_terms.astype(jnp.bfloat16), "batch").astype(jnp.float32),
        lax.psum(parent_terms.astype(jnp.bfloat16), "batch").astype(jnp.float32),
    )
    fine_stack, parent_stack = with_partners(
        fine_total.astype(jnp.bfloat16), parent_total.astype(jnp.bfloat16)
    )
    fine_far = far_field(fine_stack, fine_source, fine_operator, operators, 0)
    parent_far = far_field(parent_stack, parent_source, parent_operator, operators, 0)
    parent_local = (coarse_local + parent_far).astype(jnp.bfloat16)
    local = children(parent_local, fine_far, child_shift)
    values = lax.dot_general(
        basis, local, (((2,), (1,)), ((0,), (0,))), preferred_element_type=jnp.float32
    ).T
    slot_index = lax.iota(jnp.int32, values.shape[0])[:, None]
    return jnp.where(slot_index < counts, values, 0.0)


def solution(mesh):
    placed = (
        P("batch", "space", None),
        P("batch", "space", None),
        P("space", None),
        P(None, "space"),
        P(None, "space"),
        P(None, "space"),
        P(None, "space"),
        P(),
        P(),
        P("space", "batch", None),
        P("batch", "space"),
    )
    return jax.shard_map(
        body, mesh=mesh, in_specs=placed, out_specs=P("batch", "space"), check_vma=False
    )
```

profile of v0, /device:TPU:1, one launch (start us, length us, event | category | flops | bytes accessed | tf_op | source)
XLA Modules:
  0.0 527.7 jit_solution(15219592119479312412)
XLA Ops:
  6.5 75.3 %psum.14 = bf16[64,128]{1,0:T(8,128)(2,1)S(1)} all-reduce(bf16[64,128]{1,0:T(8,128)(2,1)} %bitcast.139), channel_id=1, replica_groups=mesh['space'=64,'batch'=8] {'batch'}, use_global_device_ids=true, to_apply=%region_0.0 | all-reduce | flops 8192 | bytes 32768 | tf_op jit(solution)/shard_map/psum | solution.py:84
  81.9 9.8 %collective-permute-start = (bf16[64,128]{1,0:T(8,128)(2,1)S(1)}, bf16[64,128]{1,0:T(8,128)(2,1)S(1)}, u32[]{:S(2)}, u32[]{:S(2)}) collective-permute-start(bf16[64,128]{1,0:T(8,128)(2,1)S(1)} %psum.14), channel_id=1, source_target_pairs={{0,8},{8,0},{16,24},{24,16},{32,40},{40,32},{48,56},{56,48},{64,72... | collective-permute-start | bytes 49160 | tf_op jit(solution)/shard_map/ppermute | solution.py:12
  94.8 4.4 collective-permute-start.2
  107.1 29.9 %while.26 = (s32[]{:T(128)}, f32[2,32,128]{2,1,0:T(8,128)}, s32[2,189,32]{1,2,0:T(8,128)}, s32[2,189,32]{1,2,0:T(8,128)}, s32[2]{0:T(128)}, /*index=5*/bf16[5,64...) while((s32[]{:T(128)}, f32[2,32,128]{2,1,0:T(8,128)}, ...), condition=%wide.region_2.3_spmd.clone, body=%wide.region_1.0_spmd.clone.sunk | while | flops 276802560 | bytes 6237277 | solution.py:45
  115.4 3.9 fusion.82
  130.3 3.9 fusion.82
  139.6 97.3 %all-reduce.2.cloned.1.call-done = bf16[512,128]{1,0:T(8,128)(2,1)} async-done(((bf16[512,128]{1,0:T(8,128)(2,1)}), bf16[512,128]{1,0:T(8,128)(2,1)}) %all-reduce.2.cloned.1.call-update) | async-done | bytes 131088 | tf_op jit(solution)/shard_map/psum | solution.py:83
  236.8 8.0 %collective-permute-start.4 = (bf16[512,128]{1,0:T(8,128)(2,1)}, bf16[512,128]{1,0:T(8,128)(2,1)S(1)}, u32[]{:S(2)}, u32[]{:S(2)}) collective-permute-start(bf16[512,128]{1,0:T(8,128)(2,1)} %all-reduce.2.cloned.1.call-done), channel_id=1, source_target_pairs={{0,8},{8,0},{16,24},{24,16},{32,40},{40,32},{48,56},{56,48},{64,72... | collective-permute-start | bytes 393224 | tf_op jit(solution)/shard_map/ppermute | solution.py:12
  248.0 4.3 collective-permute-start.6
  259.6 258.1 %while.27 = (s32[]{:T(128)}, f32[16,32,128]{2,1,0:T(8,128)}, s32[16,189,32]{1,2,0:T(8,128)}, s32[16,189,32]{1,2,0:T(8,128)}, s32[16]{0:T(128)}, /*index=5*/bf16[...) while((s32[]{:T(128)}, f32[16,32,128]{2,1,0:T(8,128)}, ...), condition=%wide.region_5.6_spmd.clone, body=%wide.region_4.5_spmd.clone.sunk | while | flops 276802560 | bytes 6237277 | solution.py:45
  269.0 3.9 fusion.89
  285.1 3.9 fusion.89
  301.3 3.9 fusion.89
  317.4 3.9 fusion.89
  333.5 3.9 fusion.89
  349.7 3.9 fusion.89
  365.8 3.9 fusion.89
  381.9 3.9 fusion.89
  398.1 3.9 fusion.89
  414.2 3.9 fusion.89
  430.3 3.9 fusion.89
  446.5 3.9 fusion.89
  478.7 3.9 fusion.89
  494.9 3.9 fusion.89
  (189 shorter events, 205.7 us)
Async XLA Ops:
  6.5 512.4 %copy-start = (bf16[512,16,128]{2,1,0:T(8,128)(2,1)S(1)}, bf16[512,16,128]{2,1,0:T(8,128)(2,1)}, u32[]{:S(2)}) copy-start(bf16[512,16,128]{2,1,0:T(8,128)(2,1)} %param.24) | copy-start | bytes 6291460
  6.5 230.3 %all-reduce.2.cloned.1.call-start = ((), (), s32[]{:S(2)}) async-start(), calls=%async_computation | async-start | bytes 262144 | tf_op jit(solution)/shard_map/psum | solution.py:83
  81.9 25.1 %collective-permute-start = (bf16[64,128]{1,0:T(8,128)(2,1)S(1)}, bf16[64,128]{1,0:T(8,128)(2,1)S(1)}, u32[]{:S(2)}, u32[]{:S(2)}) collective-permute-start(bf16[64,128]{1,0:T(8,128)(2,1)S(1)} %psum.14), channel_id=1, source_target_pairs={{0,8},{8,0},{16,24},{24,16},{32,40},{40,32},{48,56},{56,48},{64,72... | collective-permute-start | bytes 49160 | tf_op jit(solution)/shard_map/ppermute | solution.py:12
  91.7 15.3 %collective-permute-start.1 = (bf16[64,128]{1,0:T(8,128)(2,1)S(1)}, bf16[64,128]{1,0:T(8,128)(2,1)S(1)}, u32[]{:S(2)}, u32[]{:S(2)}) collective-permute-start(bf16[64,128]{1,0:T(8,128)(2,1)S(1)} %psum.14), channel_id=1, source_target_pairs={{0,16},{8,24},{16,0},{24,8},{32,48},{40,56},{48,32},{56,40},{64,80... | collective-permute-start | bytes 49160 | tf_op jit(solution)/shard_map/ppermute | solution.py:12
  94.8 12.2 %collective-permute-start.2 = (bf16[64,128]{1,0:T(8,128)(2,1)S(1)}, bf16[64,128]{1,0:T(8,128)(2,1)S(1)}, u32[]{:S(2)}, u32[]{:S(2)}) collective-permute-start(bf16[64,128]{1,0:T(8,128)(2,1)S(1)} %psum.14), channel_id=1, source_target_pairs={{0,32},{8,40},{16,48},{24,56},{32,0},{40,8},{48,16},{56,24},{64,96... | collective-permute-start | bytes 49160 | tf_op jit(solution)/shard_map/ppermute | solution.py:12
  99.2 7.9 %collective-permute-start.3 = (bf16[64,128]{1,0:T(8,128)(2,1)S(1)}, bf16[64,128]{1,0:T(8,128)(2,1)S(1)}, u32[]{:S(2)}, u32[]{:S(2)}) collective-permute-start(bf16[64,128]{1,0:T(8,128)(2,1)S(1)} %psum.14), channel_id=1, source_target_pairs={{0,64},{8,72},{16,80},{24,88},{32,96},{40,104},{48,112},{56,120},{... | collective-permute-start | bytes 49160 | tf_op jit(solution)/shard_map/ppermute | solution.py:12
  107.1 29.9 %copy-start.1 = (f32[64,128]{1,0:T(8,128)S(1)}, f32[64,128]{1,0:T(8,128)}, u32[]{:S(2)}) copy-start(f32[64,128]{1,0:T(8,128)} %param.17) | copy-start | bytes 98308
  236.8 19.3 %collective-permute-start.4 = (bf16[512,128]{1,0:T(8,128)(2,1)}, bf16[512,128]{1,0:T(8,128)(2,1)S(1)}, u32[]{:S(2)}, u32[]{:S(2)}) collective-permute-start(bf16[512,128]{1,0:T(8,128)(2,1)} %all-reduce.2.cloned.1.call-done), channel_id=1, source_target_pairs={{0,8},{8,0},{16,24},{24,16},{32,40},{40,32},{48,56},{56,48},{64,72... | collective-permute-start | bytes 393224 | tf_op jit(solution)/shard_map/ppermute | solution.py:12
  244.9 11.9 %collective-permute-start.5 = (bf16[512,128]{1,0:T(8,128)(2,1)}, bf16[512,128]{1,0:T(8,128)(2,1)S(1)}, u32[]{:S(2)}, u32[]{:S(2)}) collective-permute-start(bf16[512,128]{1,0:T(8,128)(2,1)} %all-reduce.2.cloned.1.call-done), channel_id=1, source_target_pairs={{0,16},{8,24},{16,0},{24,8},{32,48},{40,56},{48,32},{56,40},{64,80... | collective-permute-start | bytes 393224 | tf_op jit(solution)/shard_map/ppermute | solution.py:12
  248.0 9.5 %collective-permute-start.6 = (bf16[512,128]{1,0:T(8,128)(2,1)}, bf16[512,128]{1,0:T(8,128)(2,1)S(1)}, u32[]{:S(2)}, u32[]{:S(2)}) collective-permute-start(bf16[512,128]{1,0:T(8,128)(2,1)} %all-reduce.2.cloned.1.call-done), channel_id=1, source_target_pairs={{0,32},{8,40},{16,48},{24,56},{32,0},{40,8},{48,16},{56,24},{64,96... | collective-permute-start | bytes 393224 | tf_op jit(solution)/shard_map/ppermute | solution.py:12
  252.3 6.6 %collective-permute-start.7 = (bf16[512,128]{1,0:T(8,128)(2,1)}, bf16[512,128]{1,0:T(8,128)(2,1)S(1)}, u32[]{:S(2)}, u32[]{:S(2)}) collective-permute-start(bf16[512,128]{1,0:T(8,128)(2,1)} %all-reduce.2.cloned.1.call-done), channel_id=1, source_target_pairs={{0,64},{8,72},{16,80},{24,88},{32,96},{40,104},{48,112},{56,120},{... | collective-permute-start | bytes 393224 | tf_op jit(solution)/shard_map/ppermute | solution.py:12
  517.7 2.5 copy-start.2
Sparse Core Ops, SparseCore 0:
  102.0 134.8 all-reduce.1
where the time goes:
time: 532 us; the launch traced here: 528 us
  matrix products  123 us (23%)
  waiting for transfers between devices  98 us (18%)
  blocking collectives  75.3 us (14%)
  other arithmetic  72.8 us (14%)
  local copies, waits for them, and re-layouts  60.8 us (11%)
  loops' own time  46.5 us (9%)
  starting transfers between devices  37.6 us (7%)
  between operations  13.5 us (3%)
    psum x1, waiting for transfers between devices, body(): lax.psum(fine_terms.astype(jnp.bfloat16), 'batch').astype(jnp.float32)  97.3 us
    psum x1, blocking collectives, body(): lax.psum(parent_terms.astype(jnp.bfloat16), 'batch').astype(jnp.float32)  75.3 us
    dot_general x18, matrix products, one_piece(): jnp.einsum('btr,rk->btk', counted, nearby, preferred_element_type=jnp.flo...  70.7 us
    dot_general x18, matrix products, one_piece(): jnp.dot(grouped.reshape(piece_rows, kind_count * coef_width), flat_ops, p...  49.5 us
    another operation x2, loops' own time, far_field(): lax.map(one_piece, (source_pieces, kind_pieces, starts))  46.5 us
    eq x18, other arithmetic, one_piece(): chosen = (sources[:, :, None] == column_iota).astype(jnp.bfloat16)  42.6 us
    dynamic_slice x72, local copies, waits for them, and re-layouts, far_field(): lax.map(one_piece, (source_pieces, kind_pieces, starts))  39.7 us
    ppermute x8, starting transfers between devices, partner(): lax.ppermute(shard, axis, [(i, i ^ 1 << apart) for i in range(lax.axis_si...  37.6 us
  transfers between devices with their start and end apart: 9, of which 2 were waited for; matrix products, arithmetic and copies ran while one was open for 7% of the time, Pallas kernels for 0%

commit v1 on v0

--- a/solution.py
+++ b/solution.py
@@ -81,7 +81,9 @@
     parent_terms = parent_parts[0].astype(jnp.float32)
     fine_total, parent_total = (
         lax.psum(fine_terms.astype(jnp.bfloat16), "batch").astype(jnp.float32),
-        lax.psum(parent_terms.astype(jnp.bfloat16), "batch").astype(jnp.float32),
+        jnp.sum(lax.all_gather(parent_terms.astype(jnp.bfloat16), "batch"), axis=0).astype(
+            jnp.float32
+        ),
     )
     fine_stack, parent_stack = with_partners(
         fine_total.astype(jnp.bfloat16), parent_total.astype(jnp.bfloat16)

time: 532 us -> 416 us (0.78)
  other arithmetic: 72.8 us -> 1.82 us
  matrix products: 123 us -> 82.7 us
  waiting for transfers between devices: 98 us -> 128 us
  local copies, waits for them, and re-layouts: 60.8 us -> 41.1 us
  blocking collectives: 75.3 us -> 62.1 us
    psum x1 -> x0, blocking collectives: 75.3 us -> none  [body(): lax.psum(parent_terms.astype(jnp.bfloat16), 'batch').astype(jnp.float32)]
    eq x36 -> x0, other arithmetic: 69 us -> none  [the longest x18 42.6 us: one_piece(): chosen = (sources[:, :, None] == column_iota).astype(jnp.bfloat16)]
    all_gather x0 -> x1, blocking collectives: none -> 62.1 us  [body(): lax.all_gather(parent_terms.astype(jnp.bfloat16), 'batch')]
    dot_general x18, matrix products: 70.7 us -> 31.5 us  [one_piece(): jnp.einsum('btr,rk->btk', counted, nearby, preferred_element_type=jnp.flo...]
    dynamic_slice x72 -> x18, local copies, waits for them, and re-layouts: 39.7 us -> 11 us  [far_field(): lax.map(one_piece, (source_pieces, kind_pieces, starts))]
    psum x1, waiting for transfers between devices: 97.3 us -> 125 us  [body(): lax.psum(fine_terms.astype(jnp.bfloat16), 'batch').astype(jnp.float32)]
    eq x0 -> x18, local copies, waits for them, and re-layouts: none -> 12.2 us  [one_piece(): chosen = (sources[:, :, None] == column_iota).astype(jnp.bfloat16)]
  transfers between devices with their start and end apart: 9 -> 9, of which waited for: 2 -> 3; matrix products, arithmetic and copies ran while one was open for 7% -> 4% of each run, Pallas kernels for 0% -> 0%
where the time goes in v1:
time: 416 us; the launch traced here: 412 us
  waiting for transfers between devices  128 us (31%)
  matrix products  82.7 us (20%)
  blocking collectives  62.1 us (15%)
  loops' own time  46.3 us (11%)
  local copies, waits for them, and re-layouts  41.1 us (10%)
  starting transfers between devices  36.7 us (9%)
  between operations  13.7 us (3%)
    psum x1, waiting for transfers between devices, body(): lax.psum(fine_terms.astype(jnp.bfloat16), 'batch').astype(jnp.float32)  125 us
    all_gather x1, blocking collectives, body(): lax.all_gather(parent_terms.astype(jnp.bfloat16), 'batch')  62.1 us
    dot_general x18, matrix products, one_piece(): jnp.dot(grouped.reshape(piece_rows, kind_count * coef_width), flat_ops, p...  49 us
    another operation x2, loops' own time, far_field(): lax.map(one_piece, (source_pieces, kind_pieces, starts))  46.3 us
    ppermute x8, starting transfers between devices, partner(): lax.ppermute(shard, axis, [(i, i ^ 1 << apart) for i in range(lax.axis_si...  36.7 us
    dot_general x18, matrix products, one_piece(): jnp.einsum('btr,rk->btk', counted, nearby, preferred_element_type=jnp.flo...  31.5 us
    dynamic_slice x18, local copies, waits for them, and re-layouts, one_piece(): lax.dynamic_slice_in_dim(stacked, corner, WINDOW, 1).reshape(-1, coef_width)  12.7 us
    eq x18, local copies, waits for them, and re-layouts, one_piece(): chosen = (sources[:, :, None] == column_iota).astype(jnp.bfloat16)  12.2 us
  transfers between devices with their start and end apart: 9, of which 3 were waited for; matrix products, arithmetic and copies ran while one was open for 4% of the time, Pallas kernels for 0%

profile of v1, /device:TPU:1, one launch (start us, length us, event | category | flops | bytes accessed | tf_op | source)
XLA Modules:
  0.0 412.3 jit_solution(13964141991496572577)
XLA Ops:
  6.5 62.1 %all_gather.4 = bf16[8,64,128]{2,1,0:T(8,128)(2,1)S(1)} all-gather(bf16[1,64,128]{2,1,0:T(8,128)(2,1)} %param.16), channel_id=1, replica_groups=mesh['space'=64,'batch'=8] {'batch'}, dimensions={0}, use_global_device_ids=true | all-gather | bytes 147456 | tf_op jit(solution)/shard_map/all_gather | solution.py:84
  68.6 10.1 %collective-permute-start = (bf16[64,128]{1,0:T(8,128)(2,1)S(1)}, bf16[64,128]{1,0:T(8,128)(2,1)S(1)}, u32[]{:S(2)}, u32[]{:S(2)}) collective-permute-start(bf16[64,128]{1,0:T(8,128)(2,1)S(1)} %reduce_sum.12), channel_id=1, source_target_pairs={{0,8},{8,0},{16,24},{24,16},{32,40},{40,32},{48,56},{56,48},{64,72... | collective-permute-start | bytes 49160 | tf_op jit(solution)/shard_map/ppermute | solution.py:12
  80.7 4.3 %collective-permute-start.2 = (bf16[64,128]{1,0:T(8,128)(2,1)S(1)}, bf16[64,128]{1,0:T(8,128)(2,1)S(1)}, u32[]{:S(2)}, u32[]{:S(2)}) collective-permute-start(bf16[64,128]{1,0:T(8,128)(2,1)S(1)} %reduce_sum.12), channel_id=1, source_target_pairs={{0,32},{8,40},{16,48},{24,56},{32,0},{40,8},{48,16},{56,24},{64,96... | collective-permute-start | bytes 49160 | tf_op jit(solution)/shard_map/ppermute | solution.py:12
  91.1 14.3 %while.26 = (s32[]{:T(128)}, f32[2,32,128]{2,1,0:T(8,128)S(1)}, s32[2,189,32]{1,2,0:T(8,128)S(1)}, s32[2,189,32]{1,2,0:T(8,128)S(1)}, s32[2]{0:T(128)S(1)}, /*in...) while((s32[]{:T(128)}, f32[2,32,128]{2,1,0:T(8,128)S(1)}, ...), condition=%wide.region_2.3_spmd.clone, body=%wide.region_1.0_spmd.clone.sunk | while | flops 276802560 | bytes 3430497 | solution.py:45
  106.5 124.6 %all-reduce.2.cloned.1.call-done = bf16[512,128]{1,0:T(8,128)(2,1)} async-done(((bf16[512,128]{1,0:T(8,128)(2,1)}), bf16[512,128]{1,0:T(8,128)(2,1)}) %all-reduce.2.cloned.1.call-update) | async-done | bytes 131088 | tf_op jit(solution)/shard_map/psum | solution.py:83
  231.1 8.0 %collective-permute-start.4 = (bf16[512,128]{1,0:T(8,128)(2,1)}, bf16[512,128]{1,0:T(8,128)(2,1)S(1)}, u32[]{:S(2)}, u32[]{:S(2)}) collective-permute-start(bf16[512,128]{1,0:T(8,128)(2,1)} %all-reduce.2.cloned.1.call-done), channel_id=1, source_target_pairs={{0,8},{8,0},{16,24},{24,16},{32,40},{40,32},{48,56},{56,48},{64,72... | collective-permute-start | bytes 393224 | tf_op jit(solution)/shard_map/ppermute | solution.py:12
  239.2 3.1 collective-permute-start.5
  242.3 4.3 %collective-permute-start.6 = (bf16[512,128]{1,0:T(8,128)(2,1)}, bf16[512,128]{1,0:T(8,128)(2,1)S(1)}, u32[]{:S(2)}, u32[]{:S(2)}) collective-permute-start(bf16[512,128]{1,0:T(8,128)(2,1)} %all-reduce.2.cloned.1.call-done), channel_id=1, source_target_pairs={{0,32},{8,40},{16,48},{24,56},{32,0},{40,8},{48,16},{56,24},{64,96... | collective-permute-start | bytes 393224 | tf_op jit(solution)/shard_map/ppermute | solution.py:12
  254.0 148.4 %while.27 = (s32[]{:T(128)}, f32[16,32,128]{2,1,0:T(8,128)}, s32[16,189,32]{1,2,0:T(8,128)S(1)}, s32[16,189,32]{1,2,0:T(8,128)}, s32[16]{0:T(128)S(1)}, /*index=...) while((s32[]{:T(128)}, f32[16,32,128]{2,1,0:T(8,128)}, ...), condition=%wide.region_5.6_spmd.clone, body=%wide.region_4.5_spmd.clone.sunk | while | flops 276802560 | bytes 3431005 | solution.py:45
  260.5 2.8 fusion.60
  269.8 2.8 fusion.60
  288.3 2.8 fusion.60
  297.6 2.8 fusion.60
  306.9 2.8 fusion.60
  316.2 2.8 fusion.60
  325.4 2.8 fusion.60
  334.7 2.8 fusion.60
  344.0 2.8 fusion.60
  353.2 2.8 fusion.60
  362.5 2.8 fusion.60
  371.8 2.8 fusion.60
  381.1 2.8 fusion.60
  390.3 2.8 fusion.60
  399.6 2.8 fusion.60
  (124 shorter events, 94.0 us)
Async XLA Ops:
  6.5 397.0 %copy-start = (bf16[512,16,128]{2,1,0:T(8,128)(2,1)S(1)}, bf16[512,16,128]{2,1,0:T(8,128)(2,1)}, u32[]{:S(2)}) copy-start(bf16[512,16,128]{2,1,0:T(8,128)(2,1)} %param.24) | copy-start | bytes 6291460
  6.5 84.5 %copy-start.1 = (s32[189,64]{0,1:T(8,128)S(1)}, s32[189,64]{0,1:T(8,128)}, u32[]{:S(2)}) copy-start(s32[189,64]{0,1:T(8,128)} %param.21) | copy-start | bytes 145156
  6.5 84.5 %copy-start.2 = (s32[189,64]{0,1:T(8,128)S(1)}, s32[189,64]{0,1:T(8,128)}, u32[]{:S(2)}) copy-start(s32[189,64]{0,1:T(8,128)} %param.20) | copy-start | bytes 145156
  6.5 224.6 %all-reduce.2.cloned.1.call-start = ((), (), s32[]{:S(2)}) async-start(), calls=%async_computation | async-start | bytes 262144 | tf_op jit(solution)/shard_map/psum | solution.py:83
  68.6 22.3 %collective-permute-start = (bf16[64,128]{1,0:T(8,128)(2,1)S(1)}, bf16[64,128]{1,0:T(8,128)(2,1)S(1)}, u32[]{:S(2)}, u32[]{:S(2)}) collective-permute-start(bf16[64,128]{1,0:T(8,128)(2,1)S(1)} %reduce_sum.12), channel_id=1, source_target_pairs={{0,8},{8,0},{16,24},{24,16},{32,40},{40,32},{48,56},{56,48},{64,72... | collective-permute-start | bytes 49160 | tf_op jit(solution)/shard_map/ppermute | solution.py:12
  78.7 12.2 %collective-permute-start.1 = (bf16[64,128]{1,0:T(8,128)(2,1)S(1)}, bf16[64,128]{1,0:T(8,128)(2,1)S(1)}, u32[]{:S(2)}, u32[]{:S(2)}) collective-permute-start(bf16[64,128]{1,0:T(8,128)(2,1)S(1)} %reduce_sum.12), channel_id=1, source_target_pairs={{0,16},{8,24},{16,0},{24,8},{32,48},{40,56},{48,32},{56,40},{64,80... | collective-permute-start | bytes 49160 | tf_op jit(solution)/shard_map/ppermute | solution.py:12
  80.7 10.3 %collective-permute-start.2 = (bf16[64,128]{1,0:T(8,128)(2,1)S(1)}, bf16[64,128]{1,0:T(8,128)(2,1)S(1)}, u32[]{:S(2)}, u32[]{:S(2)}) collective-permute-start(bf16[64,128]{1,0:T(8,128)(2,1)S(1)} %reduce_sum.12), channel_id=1, source_target_pairs={{0,32},{8,40},{16,48},{24,56},{32,0},{40,8},{48,16},{56,24},{64,96... | collective-permute-start | bytes 49160 | tf_op jit(solution)/shard_map/ppermute | solution.py:12
  85.0 6.0 %collective-permute-start.3 = (bf16[64,128]{1,0:T(8,128)(2,1)S(1)}, bf16[64,128]{1,0:T(8,128)(2,1)S(1)}, u32[]{:S(2)}, u32[]{:S(2)}) collective-permute-start(bf16[64,128]{1,0:T(8,128)(2,1)S(1)} %reduce_sum.12), channel_id=1, source_target_pairs={{0,64},{8,72},{16,80},{24,88},{32,96},{40,104},{48,112},{56,120},{... | collective-permute-start | bytes 49160 | tf_op jit(solution)/shard_map/ppermute | solution.py:12
  91.1 14.3 %copy-start.4 = (f32[64,128]{1,0:T(8,128)S(1)}, f32[64,128]{1,0:T(8,128)}, u32[]{:S(2)}) copy-start(f32[64,128]{1,0:T(8,128)} %param.17) | copy-start | bytes 98308
  231.1 18.7 %collective-permute-start.4 = (bf16[512,128]{1,0:T(8,128)(2,1)}, bf16[512,128]{1,0:T(8,128)(2,1)S(1)}, u32[]{:S(2)}, u32[]{:S(2)}) collective-permute-start(bf16[512,128]{1,0:T(8,128)(2,1)} %all-reduce.2.cloned.1.call-done), channel_id=1, source_target_pairs={{0,8},{8,0},{16,24},{24,16},{32,40},{40,32},{48,56},{56,48},{64,72... | collective-permute-start | bytes 393224 | tf_op jit(solution)/shard_map/ppermute | solution.py:12
  239.2 10.7 %collective-permute-start.5 = (bf16[512,128]{1,0:T(8,128)(2,1)}, bf16[512,128]{1,0:T(8,128)(2,1)S(1)}, u32[]{:S(2)}, u32[]{:S(2)}) collective-permute-start(bf16[512,128]{1,0:T(8,128)(2,1)} %all-reduce.2.cloned.1.call-done), channel_id=1, source_target_pairs={{0,16},{8,24},{16,0},{24,8},{32,48},{40,56},{48,32},{56,40},{64,80... | collective-permute-start | bytes 393224 | tf_op jit(solution)/shard_map/ppermute | solution.py:12
  242.3 9.1 %collective-permute-start.6 = (bf16[512,128]{1,0:T(8,128)(2,1)}, bf16[512,128]{1,0:T(8,128)(2,1)S(1)}, u32[]{:S(2)}, u32[]{:S(2)}) collective-permute-start(bf16[512,128]{1,0:T(8,128)(2,1)} %all-reduce.2.cloned.1.call-done), channel_id=1, source_target_pairs={{0,32},{8,40},{16,48},{24,56},{32,0},{40,8},{48,16},{56,24},{64,96... | collective-permute-start | bytes 393224 | tf_op jit(solution)/shard_map/ppermute | solution.py:12
  246.6 6.6 %collective-permute-start.7 = (bf16[512,128]{1,0:T(8,128)(2,1)}, bf16[512,128]{1,0:T(8,128)(2,1)S(1)}, u32[]{:S(2)}, u32[]{:S(2)}) collective-permute-start(bf16[512,128]{1,0:T(8,128)(2,1)} %all-reduce.2.cloned.1.call-done), channel_id=1, source_target_pairs={{0,64},{8,72},{16,80},{24,88},{32,96},{40,104},{48,112},{56,120},{... | collective-permute-start | bytes 393224 | tf_op jit(solution)/shard_map/ppermute | solution.py:12
  253.2 0.8 copy-start.3
  402.4 2.4 copy-start.5
Sparse Core Ops, SparseCore 0:
  87.8 143.2 all-reduce.1
